TPU v7x, 32 devices: a whole 2x2x4 slice. The times are simulated.
32 devices in a mesh: groups: 2 (over x), ctx: 8 (over z, y), fsdp: 2 (over core).
Axes of the slice: x: 2, y: 2, z: 4, core: 2. Of those that a mesh axis runs over, the one named last changes fastest.
Arguments:
- tokens: bfloat16 [4096, 4096], P(('groups', 'ctx', 'fsdp')), parts along dimension 0, may hold values from -6 to 6
- routed_index: int32 [32, 24], P(('groups', 'ctx', 'fsdp')), parts along dimension 0, may hold values from 0 to 127, as said below
- routed_count: int32 [32], P(('groups', 'ctx', 'fsdp')), parts along dimension 0, may hold values from 1 to 24, 256 in all
- router_weight: float32 [4096], replicated, may hold values from -0.09375 to 0.09375
- attn_gain: float32 [4096], replicated, may hold values from 0.5 to 2
- ffn_gain: float32 [4096], replicated, may hold values from 0.5 to 2
- w_query: bfloat16 [4096, 2048], P(None, ('ctx', 'fsdp'))
- w_keyvalue: bfloat16 [4096, 1024], P('fsdp', 'ctx')
- w_out: bfloat16 [2048, 4096], P(('ctx', 'fsdp')), may hold values from -0.125 to 0.125
- w_gate: bfloat16 [4096, 7168], P('fsdp', 'ctx'), may hold values from -0.09375 to 0.09375
- w_up: bfloat16 [4096, 7168], P('fsdp', 'ctx'), may hold values from -0.09375 to 0.09375
- w_down: bfloat16 [7168, 4096], P('ctx', 'fsdp'), may hold values from -0.0625 to 0.0625
Outputs:
- blended: bfloat16 [4096, 4096], P(('groups', 'ctx', 'fsdp')), parts along dimension 0
There are 2 independent parts, one for each index of `groups`. A program takes and returns all parts, laid end to end along the dimension named above; an argument that names none is the same for every part. Nothing has to cross between parts.
Inputs may be any that keep to these rules, and one draw needn't show every extreme that they name: `routed_index`: row s holds 24 different rows of the s-th block of 128 tokens in increasing order; its first routed_count[s] entries are the routed ones. `routed_count`: the counts add up to 256.
All inputs are finite; a program needn't handle non-finite values. No bound on the sum of `routed_count` on one device may be relied on, other than what follows from the above.
Results may differ from a plain program's by a relative error of at most 0.0035.
Values may be sent and summed in bfloat16 or wider, within the bound.
A program may use at most 128 MiB of HBM per device.

v0:
```python
import math

import jax
import jax.numpy as jnp
from jax import lax
from jax.sharding import PartitionSpec as P


def from_partner(block, axis, stride):
    count = lax.axis_size(axis)
    route = []
    for low in range(count):
        high = low | 1 << stride
        if high != low and high < count:
            route += [(low, high), (high, low)]
    return lax.ppermute(block, axis, route)


def rms_norm(values, gain):
    scale = lax.rsqrt(jnp.mean(values * values, axis=-1, keepdims=True) + 1e-05)
    return (values * scale * gain).astype(jnp.bfloat16)


def rotate(block, position):
    width = block.shape[-1]
    half = width // 2
    freq = jnp.exp(-math.log(500000.0) * jnp.arange(half, dtype=jnp.float32) * 2.0 / width)
    angle = position.astype(jnp.float32)[:, None, None] * freq[None, None, :]
    cosine = jnp.cos(angle)
    sine = jnp.sin(angle)
    first = block[..., :half]
    second = block[..., half:]
    return jnp.concatenate(
        [first * cosine - second * sine, second * cosine + first * sine], axis=-1
    )


def attend(rows, position, live, attn_gain, w_query, w_keyvalue):
    normed = rms_norm(rows.astype(jnp.float32), attn_gain)
    projected_query = jnp.dot(normed, w_query, preferred_element_type=jnp.float32)
    query = rotate(projected_query[:, None, :], position)[:, 0].astype(jnp.bfloat16)
    parity = lax.axis_index("ctx") % 2
    partner = from_partner(w_keyvalue, "ctx", 0)
    mine, theirs = (
        lax.all_gather(w_keyvalue, "fsdp", axis=0, tiled=True),
        lax.all_gather(partner, "fsdp", axis=0, tiled=True),
    )
    key_weight = jnp.where(parity == 0, mine, theirs)
    value_weight = jnp.where(parity == 0, theirs, mine)
    key_proj = jnp.dot(normed, key_weight, preferred_element_type=jnp.float32)
    keys = rotate(key_proj[:, None, :], position)[:, 0].astype(jnp.bfloat16)
    values = jnp.dot(normed, value_weight, preferred_element_type=jnp.float32).astype(jnp.bfloat16)
    scale = 1.0 / math.sqrt(query.shape[-1])
    scores = jnp.dot(query, keys.T, preferred_element_type=jnp.float32) * scale
    allowed = live[None, :] & (position[None, :] <= position[:, None])
    scores = jnp.where(allowed, scores, -1e30)
    top = jnp.max(scores, axis=-1, keepdims=True)
    weights = jnp.exp(scores - top)
    probs = (weights / jnp.sum(weights, axis=-1, keepdims=True)).astype(jnp.bfloat16)
    return jnp.dot(probs, values, preferred_element_type=jnp.float32).astype(jnp.bfloat16)


def head_sum(mixed, w_out):
    return lax.psum_scatter(
        jnp.dot(mixed, w_out, preferred_element_type=jnp.float32),
        ("ctx", "fsdp"),
        scatter_dimension=0,
        tiled=True,
    )


def feed_forward(resid, ffn_gain, w_gate, w_up, w_down):
    normed = rms_norm(resid, ffn_gain)
    gathered = lax.all_gather(normed, "ctx", axis=0, tiled=True)
    gate_part = jnp.dot(
        gathered,
        lax.all_gather(w_gate, "fsdp", axis=0, tiled=True),
        preferred_element_type=jnp.float32,
    )
    up_part = jnp.dot(
        gathered,
        lax.all_gather(w_up, "fsdp", axis=0, tiled=True),
        preferred_element_type=jnp.float32,
    )
    hidden = (jax.nn.silu(gate_part) * up_part).astype(jnp.bfloat16)
    down_full = lax.all_gather(w_down, "fsdp", axis=1, tiled=True)
    return lax.psum_scatter(
        jnp.dot(hidden, down_full, preferred_element_type=jnp.float32).astype(jnp.bfloat16),
        "ctx",
        scatter_dimension=0,
        tiled=True,
    ).astype(jnp.float32)


def finish(base, attention, router_weight, ffn_gain, w_gate, w_up, w_down):
    resid = base + attention
    feed = feed_forward(resid, ffn_gain, w_gate, w_up, w_down)
    router = jax.nn.sigmoid(jnp.dot(base, router_weight, precision=lax.Precision.HIGHEST))
    return (base + router[:, None] * (attention + feed)).astype(jnp.bfloat16)


def body(
    tokens,
    routed_index,
    routed_count,
    router_weight,
    attn_gain,
    ffn_gain,
    w_query,
    w_keyvalue,
    w_out,
    w_gate,
    w_up,
    w_down,
):
    tok_rows = tokens.shape[0]
    slots = routed_index.shape[1]
    index_row = routed_index[0]
    picked = jnp.take(tokens, index_row, axis=0)
    every_rows, every_index, every_count = (
        lax.all_gather(picked, ("ctx", "fsdp"), axis=0, tiled=True),
        lax.all_gather(routed_index, ("ctx", "fsdp"), axis=0, tiled=True),
        lax.all_gather(routed_count, ("ctx", "fsdp"), axis=0, tiled=True),
    )
    shards = every_index.shape[0]
    position = (jnp.arange(shards, dtype=jnp.int32)[:, None] * tok_rows + every_index).reshape(-1)
    live = (jnp.arange(slots, dtype=jnp.int32)[None, :] < every_count[:, None]).reshape(-1)
    own_live = jnp.arange(slots, dtype=jnp.int32) < routed_count[0]
    mixed = attend(every_rows, position, live, attn_gain, w_query, w_keyvalue)
    attention = head_sum(mixed, w_out)
    updated = finish(
        picked.astype(jnp.float32), attention, router_weight, ffn_gain, w_gate, w_up, w_down
    )
    fresh = jnp.where(own_live[:, None], updated, picked)
    return tokens.at[index_row].set(fresh)


def solution(mesh):
    placed = (
        P(("groups", "ctx", "fsdp"), None),
        P(("groups", "ctx", "fsdp"), None),
        P(("groups", "ctx", "fsdp")),
        P(),
        P(),
        P(),
        P(None, ("ctx", "fsdp")),
        P("fsdp", "ctx"),
        P(("ctx", "fsdp"), None),
        P("fsdp", "ctx"),
        P("fsdp", "ctx"),
        P("ctx", "fsdp"),
    )
    return jax.shard_map(
        body,
        mesh=mesh,
        in_specs=placed,
        out_specs=P(("groups", "ctx", "fsdp"), None),
        check_vma=False,
    )
```

profile of v0, /device:TPU:1, one launch (start us, length us, event | category | flops | bytes accessed | tf_op | source)
XLA Modules:
  0.0 369.1 jit_solution(18023281590533389975)
XLA Ops:
  6.5 0.0 all-gather.9.cloned.1.call-start
  6.6 1.3 copy.17
  7.9 0.7 fusion.52
  8.7 0.7 compare_and_fusion
  9.3 0.7 gather_fusion
  10.0 0.8 broadcast_select_fusion
  10.8 0.0 all-gather.9.cloned.1.call-update
  10.8 0.0 all-gather.11.cloned.1.call-start
  10.8 0.7 all-gather.11.cloned.1.call-update
  11.5 0.0 all-gather.13.cloned.1.call-start
  12.2 0.0 copy-done.19
  12.3 0.7 dynamic-slice
  12.9 0.7 dynamic-update-slice
  13.7 2.1 collective-permute-start
  15.7 19.9 %all-reduce = s32[16]{0:T(128)S(1)} all-reduce(s32[16]{0:T(128)S(1)} %dynamic-update-slice), channel_id=1, replica_groups=mesh['groups'=2,'ctx'=8,'fsdp'=2] {'ctx','fsdp'}, use_global_device_ids=true, to_apply=%add | all-reduce | flops 16 | bytes 128
  35.6 21.2 %all-gather = s32[16,1,24]{2,1,0:T(1,128)S(1)} all-gather(s32[1,1,24]{2,1,0:T(1,128)S(1)} %bitcast.48), channel_id=1, replica_groups=mesh['groups'=2,'ctx'=8,'fsdp'=2] {'ctx','fsdp'}, dimensions={0}, use_global_device_ids=true | all-gather | bytes 1632 | tf_op jit(solution)/shard_map/all_gather | solution.py:122
  56.9 0.1 broadcast_add_fusion
  56.9 0.1 le.23
  57.0 0.1 iota_compare_fusion
  57.1 0.6 lt.59
  57.7 0.6 multiply_exponential_fusion
  58.3 0.0 collective-permute-done
  58.3 0.8 copy-done.11
  59.1 0.0 all-gather.13.cloned.1.call-update
  59.2 0.0 reduce-scatter.3.cloned.1.call-start
  59.2 1.3 all-gather.9.cloned.1.call-done
  60.5 2.7 fusion
  63.2 0.0 copy-done.12
  63.2 0.1 copy-done.3
  63.3 1.1 fusion.2
  64.4 1.6 copy-done.1
  66.0 1.0 convolution_bitcast_fusion.1
  67.1 2.8 all-gather.11.cloned.1.call-done
  69.9 11.8 %all-gather.13.cloned.1.call-done = bf16[4096,128]{1,0:T(8,128)(2,1)} async-done(((bf16[2048,128]{1,0:T(8,128)(2,1)}), bf16[4096,128]{1,0:T(8,128)(2,1)}) %all-gather.13.cloned.1.call-update) | async-done | bytes 1048592 | tf_op jit(solution)/shard_map/all_gather | solution.py:46
  81.6 3.3 convolution_bitcast_fusion
  85.0 0.5 fusion.49
  85.5 0.3 fusion.55
  85.8 0.1 fusion.14
  86.0 1.0 convolution_convert_fusion.2
  87.0 3.9 %fusion.5 = f32[384,4096]{1,0:T(8,128)} fusion(bf16[128,4096]{1,0:T(8,128)(2,1)S(1)} %copy-done, bf16[384,128]{1,0:T(8,128)(2,1)S(1)} %convolution_convert_fusion.2, f32[384,384]{0,1:T(8,128)S(1)} %get-tuple-element.12, f32[384]{0:T(512)S(1)} %fusion.14, f32[384]{0:T(512)S(1)} %get-tuple-element.11), kind=kOutput, calls=%fused_computation.16 | convolution fusion | flops 440893440 | bytes 8031232 | tf_op jit(solution)/shard_map/dot_general | solution.py:65
  90.9 0.0 reduce-scatter.3.cloned.1.call-update
  90.9 0.0 copy-start.13
  91.0 0.0 all-gather.17.cloned.1.call-start
  91.0 0.5 all-gather.17.cloned.1.call-update
  91.6 0.0 all-gather.15.cloned.1.call-start
  91.6 84.8 %reduce-scatter.3.cloned.1.call-done = f32[24,4096]{1,0:T(8,128)} async-done(((f32[384,4096]{1,0:T(8,128)}), f32[24,4096]{1,0:T(8,128)}) %reduce-scatter.3.cloned.1.call-update) | async-done | bytes 393232 | tf_op jit(solution)/shard_map/reduce_scatter | solution.py:64
  176.4 1.2 multiply_reduce_fusion
  177.7 1.8 multiply_convert_fusion
  179.5 0.0 all-gather.15.cloned.1.call-update
  179.5 0.0 all-gather.19.cloned.1.call-start
  179.5 0.7 all-gather.19.cloned.1.call-update
  180.3 0.0 all-gather.21.cloned.1.call-start
  180.3 0.7 all-gather.21.cloned.1.call-update
  181.0 0.2 reduce-scatter.5.cloned.1.call-start
  181.2 15.4 %all-gather.17.cloned.1.call-done = bf16[4096,896]{1,0:T(8,128)(2,1)} async-done(((bf16[2048,896]{1,0:T(8,128)(2,1)}), bf16[4096,896]{1,0:T(8,128)(2,1)}) %all-gather.17.cloned.1.call-update) | async-done | bytes 7340048 | tf_op jit(solution)/shard_map/all_gather | solution.py:77
  196.6 46.7 %all-gather.15.cloned.1.call-done = bf16[192,4096]{1,0:T(8,128)(2,1)} async-done(((bf16[24,4096]{1,0:T(8,128)(2,1)}), bf16[192,4096]{1,0:T(8,128)(2,1)}) %all-gather.15.cloned.1.call-update) | async-done | bytes 1572880 | tf_op jit(solution)/shard_map/all_gather | solution.py:74
  243.3 6.3 %fusion.56 = f32[192,896]{1,0:T(8,128)} fusion(bf16[192,4096]{1,0:T(8,128)(2,1)} %all-gather.15.cloned.1.call-done, bf16[4096,896]{1,0:T(8,128)(2,1)} %all-gather.17.cloned.1.call-done), kind=kOutput, calls=%fused_computation.85 | convolution fusion | flops 1409286144 | bytes 9601024 | tf_op jit(solution)/shard_map/dot_general | solution.py:75
  249.6 13.4 %all-gather.19.cloned.1.call-done = bf16[4096,896]{1,0:T(8,128)(2,1)} async-done(((bf16[2048,896]{1,0:T(8,128)(2,1)}), bf16[4096,896]{1,0:T(8,128)(2,1)}) %all-gather.19.cloned.1.call-update) | async-done | bytes 7340048 | tf_op jit(solution)/shard_map/all_gather | solution.py:82
  263.0 21.1 %all-gather.21.cloned.1.call-done = bf16[896,4096]{1,0:T(8,128)(2,1)} async-done(((bf16[896,2048]{1,0:T(8,128)(2,1)}), bf16[896,4096]{1,0:T(8,128)(2,1)}) %all-gather.21.cloned.1.call-update) | async-done | bytes 7340048 | tf_op jit(solution)/shard_map/all_gather | solution.py:86
  284.1 10.1 %convolution_convert_fusion = bf16[192,4096]{1,0:T(8,128)(2,1)} fusion(bf16[896,4096]{1,0:T(8,128)(2,1)} %all-gather.21.cloned.1.call-done, bf16[192,4096]{1,0:T(8,128)(2,1)S(1)} %copy-done.17, bf16[4096,896]{1,0:T(8,128)(2,1)} %all-gather.19.cloned.1.call-done, f32[192,896]{1,0:T(8,128)} %fusion.56), kind=kOutput, calls=%fused_computation.7 | convolution fusion | flops 2820390912 | bytes 18513920 | tf_op jit(solution)/shard_map/dot_general | solution.py:88
  294.2 0.0 reduce-scatter.5.cloned.1.call-update
  294.2 0.3 fusion.9
  294.5 64.4 %reduce-scatter.5.cloned.1.call-done = bf16[24,4096]{1,0:T(8,128)(2,1)} async-done(((bf16[192,4096]{1,0:T(8,128)(2,1)}), bf16[24,4096]{1,0:T(8,128)(2,1)}) %reduce-scatter.5.cloned.1.call-update) | async-done | bytes 196624 | tf_op jit(solution)/shard_map/reduce_scatter | solution.py:87
  358.9 3.7 %scatter_custom_fusion = bf16[128,4096]{1,0:T(8,128)(2,1)} fusion(bf16[128,4096]{1,0:T(8,128)(2,1)} %copy-done.4, s32[24]{0:T(128)S(1)} %fusion.52, f32[24,4096]{1,0:T(8,128)S(1)} %copy-done.5, bf16[24,4096]{1,0:T(8,128)(2,1)} %reduce-scatter.5.cloned.1.call-done, f32[24]{0:T(128)S(1)} %fusion.9, pred[24]{0:T(512)(128)(4,1)S(1)} %iota_compare_fusion.1, ...), kind=kCustom, calls=%fused_computation.38 | custom fusion | flops 786432 | bytes 1836544 | tf_op jit(solution)/shard_map/scatter | solution.py:135
  (41 shorter events, 0.1 us)
Async XLA Ops:
  6.5 80.5 %copy-start = (bf16[128,4096]{1,0:T(8,128)(2,1)S(1)}, bf16[128,4096]{1,0:T(8,128)(2,1)}, u32[]{:S(2)}) copy-start(bf16[128,4096]{1,0:T(8,128)(2,1)} %param.20) | copy-start | bytes 3145732
  6.5 5.7 %copy-start.19 = (u32[32]{0:T(128)S(1)}, u32[32]{0:T(128)}, u32[]{:S(2)}) copy-start(u32[32]{0:T(128)} %constant.69) | copy-start | bytes 388
  6.5 29.1 %copy-start.14 = (s32[1,24]{1,0:T(1,128)S(1)}, s32[1,24]{1,0:T(1,128)}, u32[]{:S(2)}) copy-start(s32[1,24]{1,0:T(1,128)} %param.13) | copy-start | bytes 292
  6.5 7.1 %copy-start.10 = (bf16[2048,128]{1,0:T(8,128)(2,1)S(1)}, bf16[2048,128]{1,0:T(8,128)(2,1)}, u32[]{:S(2)}) copy-start(bf16[2048,128]{1,0:T(8,128)(2,1)} %param.19) | copy-start | bytes 1572868
  6.5 53.9 %all-gather.9.cloned.1.call-start = ((), (), s32[]{:S(2)}) async-start(), calls=%async_computation.2 | async-start | bytes 3342336 | tf_op jit(solution)/shard_map/all_gather | solution.py:121
  7.9 56.5 %copy-start.4 = (bf16[128,4096]{1,0:T(8,128)(2,1)}, bf16[128,4096]{1,0:T(8,128)(2,1)S(1)}, u32[]{:S(2)}) copy-start(bf16[128,4096]{1,0:T(8,128)(2,1)S(1)} %copy.17) | copy-start | bytes 3145732
  7.9 55.3 %copy-start.12 = (f32[4096]{0:T(1024)S(1)}, f32[4096]{0:T(1024)}, u32[]{:S(2)}) copy-start(f32[4096]{0:T(1024)} %param.16) | copy-start | bytes 49156
  10.8 59.1 %all-gather.11.cloned.1.call-start = ((), (), s32[]{:S(2)}) async-start(), calls=%async_computation.3 | async-start | bytes 1572864 | tf_op jit(solution)/shard_map/all_gather | solution.py:45
  11.5 70.1 %all-gather.13.cloned.1.call-start = ((), (), s32[]{:S(2)}) async-start(), calls=%async_computation.4 | async-start | bytes 1572864 | tf_op jit(solution)/shard_map/all_gather | solution.py:46
  13.7 44.7 %collective-permute-start = (bf16[2048,128]{1,0:T(8,128)(2,1)S(1)}, bf16[2048,128]{1,0:T(8,128)(2,1)S(1)}, u32[]{:S(2)}, u32[]{:S(2)}) collective-permute-start(bf16[2048,128]{1,0:T(8,128)(2,1)S(1)} %copy-done.10), channel_id=1, source_target_pairs={{0,2},{2,0},{4,6},{6,4},{8,10},{10,8},{12,14},{14,12},{1,3},{3,1},... | collective-permute-start | bytes 1572872 | tf_op jit(solution)/shard_map/ppermute | solution.py:16
  58.3 0.8 copy-start.11
  59.2 117.2 %reduce-scatter.3.cloned.1.call-start = ((), (), s32[]{:S(2)}) async-start(), calls=%async_computation.5 | async-start | bytes 6684672 | tf_op jit(solution)/shard_map/reduce_scatter | solution.py:64
  60.5 2.8 copy-start.3
  63.2 2.8 copy-start.8
  64.4 1.6 copy-start.1
  67.1 17.9 %copy-start.16 = (f32[64]{0:T(128)S(1)}, f32[64]{0:T(128)}, u32[]{:S(2)}) copy-start(f32[64]{0:T(128)} %multiply_exponential_fusion) | copy-start | bytes 772
  67.1 18.4 %copy-start.15 = (pred[384]{0:T(512)(128)(4,1)S(1)}, pred[384]{0:T(512)(128)(4,1)}, u32[]{:S(2)}) copy-start(pred[384]{0:T(512)(128)(4,1)} %lt.59) | copy-start | bytes 1156
  69.9 16.1 %copy-start.6 = (bf16[4096,128]{1,0:T(8,128)(2,1)S(1)}, bf16[4096,128]{1,0:T(8,128)(2,1)}, u32[]{:S(2)}) copy-start(bf16[4096,128]{1,0:T(8,128)(2,1)} %all-gather.11.cloned.1.call-done) | copy-start | bytes 3145732
  81.6 4.3 %copy-start.2 = (bf16[384,4096]{1,0:T(8,128)(2,1)S(1)}, bf16[384,4096]{1,0:T(8,128)(2,1)}, u32[]{:S(2)}) copy-start(bf16[384,4096]{1,0:T(8,128)(2,1)} %copy-done.1) | copy-start | bytes 9437188
  81.6 4.3 %copy-start.7 = (bf16[4096,128]{1,0:T(8,128)(2,1)S(1)}, bf16[4096,128]{1,0:T(8,128)(2,1)}, u32[]{:S(2)}) copy-start(bf16[4096,128]{1,0:T(8,128)(2,1)} %all-gather.13.cloned.1.call-done) | copy-start | bytes 3145732
  90.9 86.7 %copy-start.13 = (f32[4096]{0:T(1024)S(1)}, f32[4096]{0:T(1024)}, u32[]{:S(2)}) copy-start(f32[4096]{0:T(1024)} %param.17) | copy-start | bytes 49156
  91.0 105.6 %all-gather.17.cloned.1.call-start = ((), (), s32[]{:S(2)}) async-start(), calls=%async_computation.7 | async-start | bytes 11010048 | tf_op jit(solution)/shard_map/all_gather | solution.py:77
  91.6 151.7 %all-gather.15.cloned.1.call-start = ((), (), s32[]{:S(2)}) async-start(), calls=%async_computation.6 | async-start | bytes 1769472 | tf_op jit(solution)/shard_map/all_gather | solution.py:74
  179.5 83.5 %all-gather.19.cloned.1.call-start = ((), (), s32[]{:S(2)}) async-start(), calls=%async_computation.8 | async-start | bytes 11010048 | tf_op jit(solution)/shard_map/all_gather | solution.py:82
  180.3 103.9 %all-gather.21.cloned.1.call-start = ((), (), s32[]{:S(2)}) async-start(), calls=%async_computation.9 | async-start | bytes 11010048 | tf_op jit(solution)/shard_map/all_gather | solution.py:86
  181.0 177.9 %reduce-scatter.5.cloned.1.call-start = ((), (), s32[]{:S(2)}) async-start(), calls=%async_computation.10 | async-start | bytes 1769472 | tf_op jit(solution)/shard_map/reduce_scatter | solution.py:87
  243.2 40.9 %copy-start.17 = (bf16[192,4096]{1,0:T(8,128)(2,1)S(1)}, bf16[192,4096]{1,0:T(8,128)(2,1)}, u32[]{:S(2)}) copy-start(bf16[192,4096]{1,0:T(8,128)(2,1)} %all-gather.15.cloned.1.call-done) | copy-start | bytes 4718596
  249.6 44.7 %copy-start.9 = (bf16[24,4096]{1,0:T(8,128)(2,1)S(1)}, bf16[24,4096]{1,0:T(8,128)(2,1)}, u32[]{:S(2)}) copy-start(bf16[24,4096]{1,0:T(8,128)(2,1)} %broadcast_select_fusion) | copy-start | bytes 589828
  249.6 44.7 %copy-start.18 = (f32[4096]{0:T(1024)S(1)}, f32[4096]{0:T(1024)}, u32[]{:S(2)}) copy-start(f32[4096]{0:T(1024)} %param.15) | copy-start | bytes 49156
  249.6 109.3 %copy-start.5 = (f32[24,4096]{1,0:T(8,128)S(1)}, f32[24,4096]{1,0:T(8,128)}, u32[]{:S(2)}) copy-start(f32[24,4096]{1,0:T(8,128)} %reduce-scatter.3.cloned.1.call-done) | copy-start | bytes 1179652
Sparse Core Ops, SparseCore 0:
  10.9 49.5 all-gather.8
  62.0 7.7 all-gather.10
  71.4 10.1 all-gather.12
  91.1 85.2 reduce-scatter.2
  177.9 18.6 all-gather.16
  198.9 44.3 all-gather.14
  244.9 18.0 all-gather.18
  264.6 19.4 all-gather.20
  294.3 64.4 reduce-scatter.4
where the time goes:
time: 371 us; the launch traced here: 369 us
  waiting for transfers between devices  264 us (71%)
  blocking collectives  41.1 us (11%)
  matrix products  26.2 us (7%)
  other arithmetic  14.1 us (4%)
  between operations  14.1 us (4%)
  local copies, waits for them, and re-layouts  6.7 us (2%)
    reduce_scatter x1, waiting for transfers between devices, head_sum(): lax.psum_scatter(jnp.dot(mixed, w_out, preferred_element_type=jnp.float32...  84.8 us
    reduce_scatter x1, waiting for transfers between devices, feed_forward(): lax.psum_scatter(jnp.dot(hidden, down_full, preferred_element_type=jnp.fl...  64.4 us
    all_gather x1, waiting for transfers between devices, feed_forward(): gathered = lax.all_gather(normed, 'ctx', axis=0, tiled=True)  46.7 us
    all_gather x1, blocking collectives, body(): lax.all_gather(routed_index, ('ctx', 'fsdp'), axis=0, tiled=True)  21.2 us
    all_gather x1, waiting for transfers between devices, feed_forward(): down_full = lax.all_gather(w_down, 'fsdp', axis=1, tiled=True)  21.1 us
    unnamed x1, blocking collectives  19.9 us
    all_gather x1, waiting for transfers between devices, feed_forward(): lax.all_gather(w_gate, 'fsdp', axis=0, tiled=True)  15.4 us
    all_gather x1, waiting for transfers between devices, feed_forward(): lax.all_gather(w_up, 'fsdp', axis=0, tiled=True)  13.4 us
  transfers between devices with their start and end apart: 10, of which 9 were waited for; matrix products, arithmetic and copies ran while one was open for 5% of the time, Pallas kernels for 0%

commit v1 on v0

v1 whole, which is shorter than its diff:
```python
import functools
import math

import jax
import jax.numpy as jnp
from jax import lax
from jax.experimental import pallas as pl
from jax.experimental.pallas import tpu as pltpu
from jax.sharding import PartitionSpec as P

F32 = jnp.float32
BF16 = jnp.bfloat16
MESH = pl.DeviceIdType.MESH
CAP = 24
BLK = 48
ROW = 32
META = 128
CHUNK = 512


def dot(a, b):
    return jnp.dot(a, b, preferred_element_type=F32)


def rope(u, cosine, sine):
    return u * cosine + pltpu.roll(u, 64, 1) * sine


def kernel(
    m, d, tok_rows,
    x_ref, again_ref, fgain_ref, wq_hbm, wkv_hbm, wo_hbm, wg_hbm, wu_hbm, wd_hbm,
    out_ref,
    grid, wq, wkv, wo, wg, wu, wd,
    meta, picked, normed, kvp, kvp_in, kv, kv_in, mix,
    pb, rb, sb, tb, att, ssq, n2, gu, gu_in, hid, pc, pd, rd, sd, td, dl, dr,
    lsem, ssem, rsem,
):
    half = d // 2
    shards = 4 * m
    rows = 16 * shards
    nch = half // CHUNK
    c = lax.axis_index("ctx")
    f = lax.axis_index("fsdp")
    hi, lo = c // 2, lax.rem(c, 2)
    sib = {"fsdp": 1 - f}
    pair = {"ctx": hi * 2 + 1 - lo}

    def across(k):
        return {"ctx": lax.rem(hi + k, m) * 2 + lo}

    def source(k):
        return lax.rem(hi + m - k, m)

    taken = [0]
    sent = []

    def remote(src, dst, to):
        i = taken[0]
        taken[0] += 1
        copy = pltpu.make_async_remote_copy(
            src_ref=src, dst_ref=dst, send_sem=ssem.at[i], recv_sem=rsem.at[i],
            device_id=to, device_id_type=MESH,
        )
        copy.start()
        sent.append(copy)
        return copy

    barrier = pltpu.get_barrier_semaphore()
    for to in [sib, pair] + [across(k) for k in range(1, m)]:
        pl.semaphore_signal(barrier, inc=1, device_id=to, device_id_type=MESH)
    pl.semaphore_wait(barrier, m + 1)

    def gather(block, dest, with_sib):
        ahead = [remote(block, dest(lo, hi), across(k)) for k in range(1, m)]
        by_pair = [remote(block, dest(lo, hi), pair)]
        by_sib = []
        if with_sib:
            by_sib.append(remote(block, dest(lo, hi), sib))
        for k in range(1, m):
            ahead[k - 1].wait_recv()
            at = dest(lo, source(k))
            by_pair.append(remote(at, at, pair))
            if with_sib:
                by_sib.append(remote(at, at, sib))
        for k in range(m):
            by_pair[k].wait_recv()
            if with_sib:
                at = dest(1 - lo, source(k) if k else hi)
                by_sib.append(remote(at, at, sib))
        for copy in by_sib:
            copy.wait_recv()

    loads = []

    def load(src, dst):
        copy = pltpu.make_async_copy(src, dst, lsem.at[len(loads)])
        copy.start()
        loads.append(copy)
        return copy

    mine = pl.ds(pl.multiple_of(f * half, 128), half)
    other = pl.ds(pl.multiple_of((1 - f) * half, 128), half)
    get_wq, get_wkv = load(wq_hbm, wq), load(wkv_hbm, wkv)
    get_wo = load(wo_hbm.at[:, mine], wo.at[f])
    get_wg, get_wu, get_wd = load(wg_hbm, wg), load(wu_hbm, wu), load(wd_hbm, wd)
    grid[lo, hi, f] = x_ref[...]
    gather(x_ref, lambda a, b: grid.at[a, b, f], True)
    wo_in = remote(wo_hbm.at[:, other], wo.at[f], sib)

    total = shards * BLK
    for a in range(2):
        for b in range(m):
            for e in range(2):
                at = ((a * m + b) * 2 + e) * CAP
                meta[at:at + CAP] = grid[a, b, e, :, half:].astype(F32)[:CAP]

    def shard_of(block):
        return lax.rem(block // 2, m) * 4 + block // (2 * m) * 2 + lax.rem(block, 2)

    lanes = grid[:, :, :, :, half:].reshape(total, META).astype(F32).T
    glane = lax.broadcasted_iota(jnp.int32, (8, total), 1)
    gslot = lax.rem(glane, BLK)
    count_l = jnp.broadcast_to(lanes[1:2], (8, total))
    first = jnp.where(gslot == 0, count_l, 0.0).astype(BF16)
    tri = shard_of(lax.broadcasted_iota(jnp.int32, (total, total), 0) // BLK) < shard_of(
        lax.broadcasted_iota(jnp.int32, (total, total), 1) // BLK)
    start_l = dot(first, tri.astype(F32).astype(BF16))
    wide = gslot.astype(F32)
    left = jnp.where(wide < count_l, start_l + wide, -1.0)[:1]
    wide = wide - CAP
    right = jnp.where((wide >= 0) & (wide < count_l), start_l + wide, -1.0)[:1]
    place = lax.broadcasted_iota(jnp.int32, (rows, total), 0).astype(F32)
    left = jnp.where(left == place, 1.0, 0.0).astype(BF16)
    right = jnp.where(right == place, 1.0, 0.0).astype(BF16)

    square = jnp.zeros((rows, 1), F32)
    for h, pick in enumerate((left, right)):
        for j in range(nch):
            cut = slice(j * CHUNK, (j + 1) * CHUNK)
            got = dot(pick, grid[:, :, :, :, cut].reshape(total, CHUNK))
            square = square + jnp.sum(got * got, axis=1, keepdims=True)
            picked[h, :, cut] = got.astype(BF16)
    scale = lax.rsqrt(square / d + 1e-05)
    for h in range(2):
        for j in range(nch):
            cut = slice(j * CHUNK, (j + 1) * CHUNK)
            normed[h, :, cut] = (
                picked[h, :, cut].astype(F32) * scale * again_ref[h, :, cut]).astype(BF16)

    get_wkv.wait()
    kvp[...] = dot(normed[f], wkv[...])
    kvp_in_copy = remote(kvp, kvp_in, sib)
    info = dot(left, grid[:, :, :, :, half:].reshape(total, META))
    position = info[:, 2:3] * tok_rows + info[:, 0:1]
    lane = lax.broadcasted_iota(jnp.int32, (rows, 128), 1)
    freq = jnp.exp(-math.log(500000.0) * lax.rem(lane, 64).astype(F32) * 2.0 / 128)
    angle = position * freq
    cosine = jnp.cos(angle)
    sine = jnp.where(lane < 64, -1.0, 1.0) * jnp.sin(angle)
    get_wq.wait()
    query = rope(dot(normed[0], wq[:half]) + dot(normed[1], wq[half:]), cosine, sine).astype(BF16)
    kvp_in_copy.wait_recv()
    both = kvp[...] + kvp_in[...]
    holds_keys = lo == 0
    kv[...] = jnp.where(holds_keys, rope(both, cosine, sine), both).astype(BF16)
    kv_copy = remote(kv, kv_in, pair)
    kv_copy.wait_recv()
    keys = jnp.where(holds_keys, kv[...].astype(F32), kv_in[...].astype(F32)).astype(BF16)
    values = jnp.where(holds_keys, kv_in[...].astype(F32), kv[...].astype(F32)).astype(BF16)
    scores = lax.dot_general(query, keys, (((1,), (1,)), ((), ())), preferred_element_type=F32)
    scores = scores * (1.0 / math.sqrt(128))
    seen = lax.broadcasted_iota(jnp.int32, (rows, rows), 1) <= lax.broadcasted_iota(
        jnp.int32, (rows, rows), 0)
    scores = jnp.where(seen, scores, -1e30)
    weights = jnp.exp(scores - jnp.max(scores, axis=1, keepdims=True))
    probs = (weights / jnp.sum(weights, axis=1, keepdims=True)).astype(BF16)
    mix[f] = dot(probs, values).astype(BF16)
    mix_copy = remote(mix.at[f], mix.at[f], sib)
    get_wo.wait()
    wo_in.wait_recv()
    mix_copy.wait_recv()

    def scatter(part, order, size, pbuf, rbuf, sbuf, tbuf, take):
        passed = []
        for j in range(nch):
            value = part(j)
            for a in range(2):
                for b in range(m):
                    at = order(a, b) * size
                    pbuf[j, a, b] = value[at:at + size].astype(BF16)
            passed.append(remote(pbuf.at[j, 1 - lo], rbuf.at[j], pair))
        spread = []
        for j in range(nch):
            passed[j].wait_recv()
            sbuf[j] = (pbuf[j, lo].astype(F32) + rbuf[j].astype(F32)).astype(BF16)
            spread.append([
                remote(sbuf.at[j, lax.rem(hi + k, m)], tbuf.at[j, k - 1], across(k))
                for k in range(1, m)])
        for j in range(nch):
            whole = pbuf[j, lo, hi].astype(F32) + rbuf[j, hi].astype(F32)
            for k in range(1, m):
                spread[j][k - 1].wait_recv()
                whole = whole + tbuf[j, k - 1].astype(F32)
            take(j, whole)

    mixed = jnp.concatenate([mix[0], mix[1]], axis=1)

    def project(j):
        cut = slice(j * CHUNK, (j + 1) * CHUNK)
        return dot(mixed, wo[:, :, cut].reshape(256, CHUNK))

    own = pl.ds(pl.multiple_of(c * ROW, ROW), ROW)

    def keep(j, whole):
        att[:, j * CHUNK:(j + 1) * CHUNK] = whole

    scatter(project, lambda a, b: b * 2 + a, ROW, pb, rb, sb, tb, keep)

    resid = picked[f, own, :].astype(F32) + att[...]
    ssq[0] = jnp.broadcast_to(jnp.sum(resid * resid, axis=1, keepdims=True), (ROW, 128))
    remote(ssq.at[0], ssq.at[1], sib).wait_recv()
    scale2 = lax.rsqrt((ssq[0] + ssq[1])[:, :1] / d + 1e-05)
    n2[lo, hi] = (resid * scale2 * fgain_ref[f]).astype(BF16)
    gather(n2.at[lo, hi], lambda a, b: n2.at[a, b], False)

    get_wg.wait()
    get_wu.wait()
    ff = wg.shape[1]
    hrows = rows // 2
    away = n2[1 - f].reshape(hrows, half)
    gu[0] = dot(away, wg[...]).astype(BF16)
    gu[1] = dot(away, wu[...]).astype(BF16)
    gu_copy = remote(gu, gu_in, sib)
    home = n2[f].reshape(hrows, half)
    gate = dot(home, wg[...])
    up = dot(home, wu[...])
    gu_copy.wait_recv()
    gate = gate + gu_in[0].astype(F32)
    up = up + gu_in[1].astype(F32)
    hid[f] = (gate / (1.0 + jnp.exp(-gate)) * up).astype(BF16)
    hid_copy = remote(hid.at[f], hid.at[f], sib)

    slots = shards * CAP
    sub = lax.broadcasted_iota(jnp.int32, (slots, META), 0)
    count_s = meta[:, 1:2]
    lead = jnp.where(lax.rem(sub, CAP) == 0, meta[...], 0.0).astype(BF16)
    tri_s = shard_of(lax.broadcasted_iota(jnp.int32, (slots, slots), 1) // CAP) < shard_of(
        lax.broadcasted_iota(jnp.int32, (slots, slots), 0) // CAP)
    start_s = dot(tri_s.astype(F32).astype(BF16), lead)[:, 1:2]
    slot_s = lax.rem(sub, CAP)[:, :1].astype(F32)
    target = jnp.where(slot_s < count_s, start_s + slot_s, -1.0)
    p = lax.broadcasted_iota(jnp.int32, (slots, rows), 1)
    natural = (lax.rem(p // ROW, m) * 2 + p // (ROW * m)) * ROW + lax.rem(p, ROW)
    expand = jnp.where(target == natural.astype(F32), 1.0, 0.0).astype(BF16)

    get_wd.wait()
    hid_copy.wait_recv()
    hidden = hid[...].reshape(rows, ff)
    own_perm = pl.ds(pl.multiple_of((lo * m + hi) * ROW, ROW), ROW)

    def feed(j):
        cut = slice(j * CHUNK, (j + 1) * CHUNK)
        pc[...] = dot(hidden, wd[:, cut])
        pc[own_perm, :] += att[:, cut]
        return dot(expand, pc[...].astype(BF16))

    def deliver(j, whole):
        cut = slice(j * CHUNK, (j + 1) * CHUNK)
        dl[0, :, cut] = whole[:CAP]
        dl[1, :, cut] = whole[CAP:]

    scatter(feed, lambda a, b: a * m + b, BLK, pd, rd, sd, td, deliver)
    remote(dl.at[1 - f], dr, sib).wait_recv()
    out_ref[f] = dl[f]
    out_ref[1 - f] = dr[...]
    for copy in sent:
        copy.wait_send()


def body(
    tokens, routed_index, routed_count, router_weight, attn_gain, ffn_gain,
    w_query, w_keyvalue, w_out, w_gate, w_up, w_down,
):
    tok_rows, d = tokens.shape
    half = d // 2
    n = lax.axis_size("ctx")
    m = n // 2
    shards = 2 * n
    rows = 16 * shards
    slots = shards * CAP
    nch = half // CHUNK
    ff = w_gate.shape[1]
    index_row = routed_index[0]
    picked = jnp.take(tokens, index_row, axis=0)
    shard = lax.axis_index("ctx") * 2 + lax.axis_index("fsdp")
    lane = jnp.arange(META)[None, :]
    facts = jnp.where(
        lane == 0, index_row[:, None],
        jnp.where(lane == 1, routed_count[0], jnp.where(lane == 2, shard, 0))).astype(BF16)
    block = jnp.concatenate(
        [jnp.concatenate([picked[:, :half], facts], 1),
         jnp.concatenate([picked[:, half:], facts], 1)], 0)
    copies = 4 * m - 1 + 4 + 2 * nch * m + 1 + 2 * m - 1 + 3 + 8
    vm = pl.BlockSpec(memory_space=pltpu.VMEM)
    hbm = pl.BlockSpec(memory_space=pl.ANY)
    flops = 2 * rows * half * ff * 3
    delta = pl.pallas_call(
        functools.partial(kernel, m, d, tok_rows),
        out_shape=jax.ShapeDtypeStruct((2, CAP, half), F32),
        in_specs=[vm] * 3 + [hbm] * 6,
        out_specs=vm,
        scratch_shapes=[
            pltpu.VMEM((2, m, 2, BLK, half + META), BF16),
            pltpu.VMEM(w_query.shape, BF16),
            pltpu.VMEM(w_keyvalue.shape, BF16),
            pltpu.VMEM((2, 128, half), BF16),
            pltpu.VMEM(w_gate.shape, BF16),
            pltpu.VMEM(w_up.shape, BF16),
            pltpu.VMEM(w_down.shape, BF16),
            pltpu.VMEM((slots, META), F32),
            pltpu.VMEM((2, rows, half), BF16),
            pltpu.VMEM((2, rows, half), BF16),
            pltpu.VMEM((rows, 128), F32),
            pltpu.VMEM((rows, 128), F32),
            pltpu.VMEM((rows, 128), BF16),
            pltpu.VMEM((rows, 128), BF16),
            pltpu.VMEM((2, rows, 128), BF16),
            pltpu.VMEM((nch, 2, m, ROW, CHUNK), BF16),
            pltpu.VMEM((nch, m, ROW, CHUNK), BF16),
            pltpu.VMEM((nch, m, ROW, CHUNK), BF16),
            pltpu.VMEM((nch, m - 1, ROW, CHUNK), BF16),
            pltpu.VMEM((ROW, half), F32),
            pltpu.VMEM((2, ROW, 128), F32),
            pltpu.VMEM((2, m, ROW, half), BF16),
            pltpu.VMEM((2, rows // 2, ff), BF16),
            pltpu.VMEM((2, rows // 2, ff), BF16),
            pltpu.VMEM((2, rows // 2, ff), BF16),
            pltpu.VMEM((rows, CHUNK), F32),
            pltpu.VMEM((nch, 2, m, BLK, CHUNK), BF16),
            pltpu.VMEM((nch, m, BLK, CHUNK), BF16),
            pltpu.VMEM((nch, m, BLK, CHUNK), BF16),
            pltpu.VMEM((nch, m - 1, BLK, CHUNK), BF16),
            pltpu.VMEM((2, CAP, half), F32),
            pltpu.VMEM((CAP, half), F32),
            pltpu.SemaphoreType.DMA((6,)),
            pltpu.SemaphoreType.DMA((copies,)),
            pltpu.SemaphoreType.DMA((copies,)),
        ],
        compiler_params=pltpu.CompilerParams(
            collective_id=0, has_side_effects=True, vmem_limit_bytes=60 * 1024 * 1024),
        cost_estimate=pl.CostEstimate(flops=flops, bytes_accessed=14 << 20, transcendentals=0),
        name="depth_block",
    )(block, attn_gain.reshape(2, 1, half), ffn_gain.reshape(2, 1, half),
      w_query, w_keyvalue, w_out, w_gate, w_up, w_down)
    base = picked.astype(F32)
    router = jax.nn.sigmoid(jnp.dot(base, router_weight, precision=lax.Precision.HIGHEST))
    delta = jnp.concatenate([delta[0], delta[1]], axis=1)
    updated = (base + router[:, None] * delta).astype(BF16)
    live = jnp.arange(CAP, dtype=jnp.int32) < routed_count[0]
    hit = (jnp.arange(tok_rows, dtype=jnp.int32)[:, None] == index_row[None, :]) & live[None, :]
    placed = jnp.dot(hit.astype(BF16), updated, preferred_element_type=F32).astype(BF16)
    return jnp.where(jnp.any(hit, axis=1)[:, None], placed, tokens)


def solution(mesh):
    placed = (
        P(("groups", "ctx", "fsdp"), None),
        P(("groups", "ctx", "fsdp"), None),
        P(("groups", "ctx", "fsdp")),
        P(),
        P(),
        P(),
        P(None, ("ctx", "fsdp")),
        P("fsdp", "ctx"),
        P(("ctx", "fsdp"), None),
        P("fsdp", "ctx"),
        P("fsdp", "ctx"),
        P("ctx", "fsdp"),
    )
    return jax.shard_map(
        body,
        mesh=mesh,
        in_specs=placed,
        out_specs=P(("groups", "ctx", "fsdp"), None),
        check_vma=False,
    )
```

time: 371 us -> 128 us (0.35)
  waiting for transfers between devices: 264 us -> 0 us
  Pallas kernels: 0 us -> 119 us
  blocking collectives: 41.1 us -> 0 us
  matrix products: 26.2 us -> 1.79 us
  between operations: 14.1 us -> 0.72 us
  other arithmetic: 14.1 us -> 3.6 us
    reduce_scatter x2 -> x0, waiting for transfers between devices: 149 us -> none  [the longest x1 84.8 us: head_sum(): lax.psum_scatter(jnp.dot(mixed, w_out, preferred_element_type=jnp.float32...]
    pallas_call x0 -> x1, Pallas kernels: none -> 119 us  [body(): pl.pallas_call(functools.partial(kernel, m, d, tok_rows), out_shape=jax.S...]
    all_gather x7 -> x0, waiting for transfers between devices: 112 us -> none  [the longest x1 46.7 us: feed_forward(): gathered = lax.all_gather(normed, 'ctx', axis=0, tiled=True)]
    dot_general x8 -> x2, matrix products: 26.2 us -> 1.79 us  [the longest x1 1.53 us: body(): jnp.dot(hit.astype(BF16), updated, preferred_element_type=F32).astype(BF16)]
    all_gather x1 -> x0, blocking collectives: 21.2 us -> none  [body(): lax.all_gather(routed_index, ('ctx', 'fsdp'), axis=0, tiled=True)]
    unnamed x1 -> x0, blocking collectives: 19.9 us -> none
    unnamed x44 -> x6, local copies, waits for them, and re-layouts: 5.31 us -> 0.07 us
    reduce_sum x3 -> x0, other arithmetic: 4.09 us -> none  [the longest x2 3.97 us: rms_norm(): scale = lax.rsqrt(jnp.mean(values * values, axis=-1, keepdims=True) + 1e-05)]
  transfers between devices with their start and end apart: 10 -> 0, of which waited for: 9 -> 0; matrix products, arithmetic and copies ran while one was open for 5% -> 0% of each run, Pallas kernels for 0% -> 0%
where the time goes in v1:
time: 128 us
  Pallas kernels  119 us (93%)
  other arithmetic  3.6 us (3%)
  local copies, waits for them, and re-layouts  3.37 us (3%)
  matrix products  1.79 us (1%)
    pallas_call x1, Pallas kernels, body(): pl.pallas_call(functools.partial(kernel, m, d, tok_rows), out_shape=jax.S...  119 us

profile of v1, /device:TPU:1, one launch (start us, length us, event | category | flops | bytes accessed | tf_op | source)
XLA Modules:
  0.0 128.0 jit_solution(1252209684182305293)
XLA Ops:
  0.0 0.0 copy-start
  0.7 0.1 copy-done
  0.7 0.7 fusion.11
  1.5 0.7 compare_and_fusion
  2.1 0.7 fusion.14
  2.8 0.7 select_convert_fusion
  3.6 2.2 %gather_fusion = bf16[24,4096]{1,0:T(8,128)(2,1)S(1)} fusion(bf16[128,4096]{1,0:T(8,128)(2,1)} %param.12, s32[1024]{0:T(1024)S(1)} %pad_clamp_fusion), kind=kCustom, calls=%fused_computation | custom fusion | bytes 393312 | tf_op jit(solution)/shard_map/jit(_take)/gather | solution.py:294
  5.8 0.1 broadcast_select_fusion
  5.9 0.3 fusion.4
  6.2 0.7 maximum_maximum_fusion.x_ref
  6.9 0.0 copy-start.1
  6.9 0.0 copy-start.2
  6.9 118.5 %depth_block.1 = f32[2,24,2048]{2,1,0:T(8,128)} custom-call(bf16[48,2176]{1,0:T(8,128)(2,1)} %maximum_maximum_fusion.x_ref, f32[2,1,2048]{2,1,0:T(1,128)} %bitcast.29, f32[2,1,2048]{2,1,0:T(1,128)} %bitcast.30, bf16[4096,128]{1,0:T(8,128)(2,1)} %wq_hbm.1, bf16[2048,128]{1,0:T(8,128)(2,1)} %wkv_hbm.1, bf16[128,4096]{1,0:T(8,128)(2,1)} %wo_hbm.1, ...), custom_call_target="tpu_custom_call" | custom-call | flops 2818572288 | bytes 14680064 | tf_op jit(solution)/shard_map/depth_block/pallas_call | solution.py:307
  125.4 1.0 slice_bitcast_fusion.1
  126.5 0.0 copy-done.1
  126.5 0.0 copy-done.2
  126.5 1.5 %fusion = bf16[128,4096]{1,0:T(8,128)(2,1)} fusion(bf16[128,4096]{1,0:T(8,128)(2,1)S(1)} %copy-done.1, pred[128]{0:T(512)(128)(4,1)S(1)} %fusion.11, f32[24,2048]{1,0:T(8,128)S(1)} %get-tuple-element.6, f32[24,2048]{1,0:T(8,128)S(1)} %get-tuple-element.5, bf16[24,4096]{1,0:T(8,128)(2,1)S(1)} %broadcast_select_fusion, f32[24]{0:T(128)S(1)} %fusion.4, ...), kind=kOutput, calls=%fused_computation.2 | convolution fusion | flops 26712064 | bytes 2687320 | tf_op jit(solution)/shard_map/dot_general | solution.py:361
  (5 shorter events, 0.1 us)
Async XLA Ops:
  0.0 0.7 copy-start
  6.9 119.6 %copy-start.1 = (bf16[128,4096]{1,0:T(8,128)(2,1)S(1)}, bf16[128,4096]{1,0:T(8,128)(2,1)}, u32[]{:S(2)}) copy-start(bf16[128,4096]{1,0:T(8,128)(2,1)} %param.12) | copy-start | bytes 3145732
  6.9 119.6 %copy-start.2 = (s32[1,24]{1,0:T(1,128)S(1)}, s32[1,24]{1,0:T(1,128)}, u32[]{:S(2)}) copy-start(s32[1,24]{1,0:T(1,128)} %param.13) | copy-start | bytes 292

commit v2 on v1

--- a/solution.py
+++ b/solution.py
@@ -16,6 +16,8 @@
 ROW = 32
 META = 128
 CHUNK = 512
+SUM = 256
+PIECES = 4
 
 
 def dot(a, b):
@@ -70,25 +72,37 @@
         pl.semaphore_signal(barrier, inc=1, device_id=to, device_id_type=MESH)
     pl.semaphore_wait(barrier, m + 1)
 
-    def gather(block, dest, with_sib):
-        ahead = [remote(block, dest(lo, hi), across(k)) for k in range(1, m)]
-        by_pair = [remote(block, dest(lo, hi), pair)]
-        by_sib = []
-        if with_sib:
-            by_sib.append(remote(block, dest(lo, hi), sib))
-        for k in range(1, m):
-            ahead[k - 1].wait_recv()
-            at = dest(lo, source(k))
-            by_pair.append(remote(at, at, pair))
+    def gather(block, dest, width, with_sib, between):
+        size = half // PIECES
+        cuts = [pl.ds(p * size, size if p < PIECES - 1 else width - p * size)
+                for p in range(PIECES)]
+        ahead, by_pair, by_sib = [], [], []
+        for cut in cuts:
+            near = dest(lo, hi).at[:, cut]
+            ahead.append([remote(block.at[:, cut], near, across(k)) for k in range(1, m)])
+            by_pair.append([remote(block.at[:, cut], near, pair)])
             if with_sib:
-                by_sib.append(remote(at, at, sib))
-        for k in range(m):
-            by_pair[k].wait_recv()
-            if with_sib:
-                at = dest(1 - lo, source(k) if k else hi)
-                by_sib.append(remote(at, at, sib))
+                by_sib.append(remote(block.at[:, cut], near, sib))
+        between()
+        for p, cut in enumerate(cuts):
+            for k in range(1, m):
+                ahead[p][k - 1].wait_recv()
+                at = dest(lo, source(k)).at[:, cut]
+                by_pair[p].append(remote(at, at, pair))
+                if with_sib:
+                    by_sib.append(remote(at, at, sib))
+            if p:
+                drain(p - 1, cuts[p - 1], dest, by_pair, by_sib, with_sib)
+        drain(PIECES - 1, cuts[-1], dest, by_pair, by_sib, with_sib)
         for copy in by_sib:
             copy.wait_recv()
+
+    def drain(p, cut, dest, by_pair, by_sib, with_sib):
+        for k in range(m):
+            by_pair[p][k].wait_recv()
+            if with_sib:
+                at = dest(1 - lo, source(k) if k else hi).at[:, cut]
+                by_sib.append(remote(at, at, sib))
 
     loads = []
 
@@ -104,27 +118,33 @@
     get_wo = load(wo_hbm.at[:, mine], wo.at[f])
     get_wg, get_wu, get_wd = load(wg_hbm, wg), load(wu_hbm, wu), load(wd_hbm, wd)
     grid[lo, hi, f] = x_ref[...]
-    gather(x_ref, lambda a, b: grid.at[a, b, f], True)
+    total = shards * BLK
+    slots = shards * CAP
+    held = []
+
+    def shard_of(block):
+        return lax.rem(block // 2, m) * 4 + block // (2 * m) * 2 + lax.rem(block, 2)
+
+    def tables():
+        down = shard_of(lax.broadcasted_iota(jnp.int32, (total, 1), 0) // BLK)
+        along = shard_of(lax.broadcasted_iota(jnp.int32, (1, total), 1) // BLK)
+        held.append((down < along).astype(F32).astype(BF16))
+
+    gather(x_ref, lambda a, b: grid.at[a, b, f], half + META, True, tables)
     wo_in = remote(wo_hbm.at[:, other], wo.at[f], sib)
 
-    total = shards * BLK
     for a in range(2):
         for b in range(m):
             for e in range(2):
                 at = ((a * m + b) * 2 + e) * CAP
                 meta[at:at + CAP] = grid[a, b, e, :, half:].astype(F32)[:CAP]
 
-    def shard_of(block):
-        return lax.rem(block // 2, m) * 4 + block // (2 * m) * 2 + lax.rem(block, 2)
-
     lanes = grid[:, :, :, :, half:].reshape(total, META).astype(F32).T
     glane = lax.broadcasted_iota(jnp.int32, (8, total), 1)
     gslot = lax.rem(glane, BLK)
     count_l = jnp.broadcast_to(lanes[1:2], (8, total))
     first = jnp.where(gslot == 0, count_l, 0.0).astype(BF16)
-    tri = shard_of(lax.broadcasted_iota(jnp.int32, (total, total), 0) // BLK) < shard_of(
-        lax.broadcasted_iota(jnp.int32, (total, total), 1) // BLK)
-    start_l = dot(first, tri.astype(F32).astype(BF16))
+    start_l = dot(first, held[0])
     wide = gslot.astype(F32)
     left = jnp.where(wide < count_l, start_l + wide, -1.0)[:1]
     wide = wide - CAP
@@ -182,7 +202,7 @@
 
     def scatter(part, order, size, pbuf, rbuf, sbuf, tbuf, take):
         passed = []
-        for j in range(nch):
+        for j in range(half // SUM):
             value = part(j)
             for a in range(2):
                 for b in range(m):
@@ -190,13 +210,13 @@
                     pbuf[j, a, b] = value[at:at + size].astype(BF16)
             passed.append(remote(pbuf.at[j, 1 - lo], rbuf.at[j], pair))
         spread = []
-        for j in range(nch):
+        for j in range(half // SUM):
             passed[j].wait_recv()
             sbuf[j] = (pbuf[j, lo].astype(F32) + rbuf[j].astype(F32)).astype(BF16)
             spread.append([
                 remote(sbuf.at[j, lax.rem(hi + k, m)], tbuf.at[j, k - 1], across(k))
                 for k in range(1, m)])
-        for j in range(nch):
+        for j in range(half // SUM):
             whole = pbuf[j, lo, hi].astype(F32) + rbuf[j, hi].astype(F32)
             for k in range(1, m):
                 spread[j][k - 1].wait_recv()
@@ -206,13 +226,13 @@
     mixed = jnp.concatenate([mix[0], mix[1]], axis=1)
 
     def project(j):
-        cut = slice(j * CHUNK, (j + 1) * CHUNK)
-        return dot(mixed, wo[:, :, cut].reshape(256, CHUNK))
+        cut = slice(j * SUM, (j + 1) * SUM)
+        return dot(mixed, wo[:, :, cut].reshape(256, SUM))
 
     own = pl.ds(pl.multiple_of(c * ROW, ROW), ROW)
 
     def keep(j, whole):
-        att[:, j * CHUNK:(j + 1) * CHUNK] = whole
+        att[:, j * SUM:(j + 1) * SUM] = whole
 
     scatter(project, lambda a, b: b * 2 + a, ROW, pb, rb, sb, tb, keep)
 
@@ -221,7 +241,21 @@
     remote(ssq.at[0], ssq.at[1], sib).wait_recv()
     scale2 = lax.rsqrt((ssq[0] + ssq[1])[:, :1] / d + 1e-05)
     n2[lo, hi] = (resid * scale2 * fgain_ref[f]).astype(BF16)
-    gather(n2.at[lo, hi], lambda a, b: n2.at[a, b], False)
+    def expansion():
+        sub = lax.broadcasted_iota(jnp.int32, (slots, META), 0)
+        count_s = meta[:, 1:2]
+        lead = jnp.where(lax.rem(sub, CAP) == 0, meta[...], 0.0).astype(BF16)
+        tri_s = shard_of(lax.broadcasted_iota(jnp.int32, (1, slots), 1) // CAP) < shard_of(
+            lax.broadcasted_iota(jnp.int32, (slots, 1), 0) // CAP)
+        start_s = dot(tri_s.astype(F32).astype(BF16), lead)[:, 1:2]
+        slot_s = lax.rem(sub, CAP)[:, :1].astype(F32)
+        target = jnp.where(slot_s < count_s, start_s + slot_s, -1.0)
+        p = lax.broadcasted_iota(jnp.int32, (1, rows), 1)
+        natural = (lax.rem(p // ROW, m) * 2 + p // (ROW * m)) * ROW + lax.rem(p, ROW)
+        held.append(jnp.where(target == natural.astype(F32), 1.0, 0.0).astype(BF16))
+
+    gather(n2.at[lo, hi], lambda a, b: n2.at[a, b], half, False, expansion)
+    expand = held[1]
 
     get_wg.wait()
     get_wu.wait()
@@ -240,32 +274,19 @@
     hid[f] = (gate / (1.0 + jnp.exp(-gate)) * up).astype(BF16)
     hid_copy = remote(hid.at[f], hid.at[f], sib)
 
-    slots = shards * CAP
-    sub = lax.broadcasted_iota(jnp.int32, (slots, META), 0)
-    count_s = meta[:, 1:2]
-    lead = jnp.where(lax.rem(sub, CAP) == 0, meta[...], 0.0).astype(BF16)
-    tri_s = shard_of(lax.broadcasted_iota(jnp.int32, (slots, slots), 1) // CAP) < shard_of(
-        lax.broadcasted_iota(jnp.int32, (slots, slots), 0) // CAP)
-    start_s = dot(tri_s.astype(F32).astype(BF16), lead)[:, 1:2]
-    slot_s = lax.rem(sub, CAP)[:, :1].astype(F32)
-    target = jnp.where(slot_s < count_s, start_s + slot_s, -1.0)
-    p = lax.broadcasted_iota(jnp.int32, (slots, rows), 1)
-    natural = (lax.rem(p // ROW, m) * 2 + p // (ROW * m)) * ROW + lax.rem(p, ROW)
-    expand = jnp.where(target == natural.astype(F32), 1.0, 0.0).astype(BF16)
-
     get_wd.wait()
     hid_copy.wait_recv()
     hidden = hid[...].reshape(rows, ff)
     own_perm = pl.ds(pl.multiple_of((lo * m + hi) * ROW, ROW), ROW)
 
     def feed(j):
-        cut = slice(j * CHUNK, (j + 1) * CHUNK)
+        cut = slice(j * SUM, (j + 1) * SUM)
         pc[...] = dot(hidden, wd[:, cut])
         pc[own_perm, :] += att[:, cut]
         return dot(expand, pc[...].astype(BF16))
 
     def deliver(j, whole):
-        cut = slice(j * CHUNK, (j + 1) * CHUNK)
+        cut = slice(j * SUM, (j + 1) * SUM)
         dl[0, :, cut] = whole[:CAP]
         dl[1, :, cut] = whole[CAP:]
 
@@ -288,7 +309,7 @@
     shards = 2 * n
     rows = 16 * shards
     slots = shards * CAP
-    nch = half // CHUNK
+    nch = half // SUM
     ff = w_gate.shape[1]
     index_row = routed_index[0]
     picked = jnp.take(tokens, index_row, axis=0)
@@ -300,7 +321,7 @@
     block = jnp.concatenate(
         [jnp.concatenate([picked[:, :half], facts], 1),
          jnp.concatenate([picked[:, half:], facts], 1)], 0)
-    copies = 4 * m - 1 + 4 + 2 * nch * m + 1 + 2 * m - 1 + 3 + 8
+    copies = PIECES * (6 * m) + 2 * nch * m + 8
     vm = pl.BlockSpec(memory_space=pltpu.VMEM)
     hbm = pl.BlockSpec(memory_space=pl.ANY)
     flops = 2 * rows * half * ff * 3
@@ -325,21 +346,21 @@
             pltpu.VMEM((rows, 128), BF16),
             pltpu.VMEM((rows, 128), BF16),
             pltpu.VMEM((2, rows, 128), BF16),
-            pltpu.VMEM((nch, 2, m, ROW, CHUNK), BF16),
-            pltpu.VMEM((nch, m, ROW, CHUNK), BF16),
-            pltpu.VMEM((nch, m, ROW, CHUNK), BF16),
-            pltpu.VMEM((nch, m - 1, ROW, CHUNK), BF16),
+            pltpu.VMEM((nch, 2, m, ROW, SUM), BF16),
+            pltpu.VMEM((nch, m, ROW, SUM), BF16),
+            pltpu.VMEM((nch, m, ROW, SUM), BF16),
+            pltpu.VMEM((nch, m - 1, ROW, SUM), BF16),
             pltpu.VMEM((ROW, half), F32),
             pltpu.VMEM((2, ROW, 128), F32),
             pltpu.VMEM((2, m, ROW, half), BF16),
             pltpu.VMEM((2, rows // 2, ff), BF16),
             pltpu.VMEM((2, rows // 2, ff), BF16),
             pltpu.VMEM((2, rows // 2, ff), BF16),
-            pltpu.VMEM((rows, CHUNK), F32),
-            pltpu.VMEM((nch, 2, m, BLK, CHUNK), BF16),
-            pltpu.VMEM((nch, m, BLK, CHUNK), BF16),
-            pltpu.VMEM((nch, m, BLK, CHUNK), BF16),
-            pltpu.VMEM((nch, m - 1, BLK, CHUNK), BF16),
+            pltpu.VMEM((rows, SUM), F32),
+            pltpu.VMEM((nch, 2, m, BLK, SUM), BF16),
+            pltpu.VMEM((nch, m, BLK, SUM), BF16),
+            pltpu.VMEM((nch, m, BLK, SUM), BF16),
+            pltpu.VMEM((nch, m - 1, BLK, SUM), BF16),
             pltpu.VMEM((2, CAP, half), F32),
             pltpu.VMEM((CAP, half), F32),
             pltpu.SemaphoreType.DMA((6,)),

time: 128 us -> 121 us (0.945)
  Pallas kernels: 119 us -> 111 us
    pallas_call x1, Pallas kernels: 119 us -> 111 us  [body(): pl.pallas_call(functools.partial(kernel, m, d, tok_rows), out_shape=jax.S...]
where the time goes in v2:
time: 121 us; the launch traced here: 120 us
  Pallas kernels  111 us (92%)
  other arithmetic  3.6 us (3%)
  local copies, waits for them, and re-layouts  3.37 us (3%)
  matrix products  1.79 us (1%)
    pallas_call x1, Pallas kernels, body(): pl.pallas_call(functools.partial(kernel, m, d, tok_rows), out_shape=jax.S...  111 us

profile of v2, /device:TPU:1, one launch (start us, length us, event | category | flops | bytes accessed | tf_op | source)
XLA Modules:
  0.0 120.3 jit_solution(989619373960027394)
XLA Ops:
  0.0 0.0 copy-start
  0.7 0.1 copy-done
  0.7 0.7 fusion.11
  1.5 0.7 compare_and_fusion
  2.1 0.7 fusion.14
  2.8 0.7 select_convert_fusion
  3.6 2.2 %gather_fusion = bf16[24,4096]{1,0:T(8,128)(2,1)S(1)} fusion(bf16[128,4096]{1,0:T(8,128)(2,1)} %param.12, s32[1024]{0:T(1024)S(1)} %pad_clamp_fusion), kind=kCustom, calls=%fused_computation | custom fusion | bytes 393312 | tf_op jit(solution)/shard_map/jit(_take)/gather | solution.py:315
  5.8 0.1 broadcast_select_fusion
  5.9 0.3 fusion.4
  6.2 0.7 maximum_maximum_fusion.x_ref
  6.9 0.0 copy-start.1
  6.9 0.0 copy-start.2
  6.9 110.8 %depth_block.1 = f32[2,24,2048]{2,1,0:T(8,128)} custom-call(bf16[48,2176]{1,0:T(8,128)(2,1)} %maximum_maximum_fusion.x_ref, f32[2,1,2048]{2,1,0:T(1,128)} %bitcast.29, f32[2,1,2048]{2,1,0:T(1,128)} %bitcast.30, bf16[4096,128]{1,0:T(8,128)(2,1)} %wq_hbm.1, bf16[2048,128]{1,0:T(8,128)(2,1)} %wkv_hbm.1, bf16[128,4096]{1,0:T(8,128)(2,1)} %wo_hbm.1, ...), custom_call_target="tpu_custom_call" | custom-call | flops 2818572288 | bytes 14680064 | tf_op jit(solution)/shard_map/depth_block/pallas_call | solution.py:328
  117.7 1.0 slice_bitcast_fusion.1
  118.7 0.0 copy-done.1
  118.8 0.0 copy-done.2
  118.8 1.5 %fusion = bf16[128,4096]{1,0:T(8,128)(2,1)} fusion(bf16[128,4096]{1,0:T(8,128)(2,1)S(1)} %copy-done.1, pred[128]{0:T(512)(128)(4,1)S(1)} %fusion.11, f32[24,2048]{1,0:T(8,128)S(1)} %get-tuple-element.6, f32[24,2048]{1,0:T(8,128)S(1)} %get-tuple-element.5, bf16[24,4096]{1,0:T(8,128)(2,1)S(1)} %broadcast_select_fusion, f32[24]{0:T(128)S(1)} %fusion.4, ...), kind=kOutput, calls=%fused_computation.2 | convolution fusion | flops 26712064 | bytes 2687320 | tf_op jit(solution)/shard_map/dot_general | solution.py:382
  (5 shorter events, 0.1 us)
Async XLA Ops:
  0.0 0.7 copy-start
  6.9 111.9 %copy-start.1 = (bf16[128,4096]{1,0:T(8,128)(2,1)S(1)}, bf16[128,4096]{1,0:T(8,128)(2,1)}, u32[]{:S(2)}) copy-start(bf16[128,4096]{1,0:T(8,128)(2,1)} %param.12) | copy-start | bytes 3145732
  6.9 111.9 %copy-start.2 = (s32[1,24]{1,0:T(1,128)S(1)}, s32[1,24]{1,0:T(1,128)}, u32[]{:S(2)}) copy-start(s32[1,24]{1,0:T(1,128)} %param.13) | copy-start | bytes 292
